TPU v7x, 32 devices: a whole 2x2x4 slice. The times are simulated.
32 devices in a mesh: aux: 8 (over z, y), occ: 4 (over x, core).
Axes of the slice: x: 2, y: 2, z: 4, core: 2. Of those that a mesh axis runs over, the one named last changes fastest.
Arguments:
- integrals: bfloat16 [128, 32, 16384], P('aux', 'occ'), may hold values from -6 to 6
- metric_factor: bfloat16 [256, 8], P(('aux', 'occ')), may hold values from -2 to 2
- coefficients: bfloat16 [2048, 128], P(None, 'occ'), may hold values from -0.5 to 0.5
- owners: int32 [128, 1], replicated, may hold values from 0 to 7; in each aligned block of 16 rows (0 to 15, 16 to 31, ...) at most 2 rows name the same one
- row_block: int32 [128], replicated, may hold values from 0 to 1
- column_block: int32 [128], replicated, may hold values from 0 to 15
- screen_counts: int32 [128], replicated, may hold values from 1 to 8
Outputs:
- exchange_blocks: float32 [16, 16384], P('aux')
Inputs may be any that keep to these rules, and one draw needn't show every extreme that they name: `owners`: in each aligned block of 16 rows (the pair blocks of one auxiliary device) no owner is named more than 2 times, a bound that some block reaches.
All inputs are finite; a program needn't handle non-finite values.
Results may differ from a plain program's by a relative error of at most 0.0011.
Values may be sent and summed in bfloat16 or wider, within the bound.
A program may use at most 128 MiB of HBM per device.

v0:
```python
import jax
import jax.numpy as jnp
from jax import lax
from jax.sharding import PartitionSpec as P

BF = 128
CAP = 2
NBLK_DEV = 2


def fit_slab(integrals, metric_factor, local_counts):
    aux_local = integrals.shape[1]
    live_rows = jnp.arange(aux_local, dtype=jnp.int32)[None, :] < local_counts[:, None]
    masked = jnp.where(live_rows[:, :, None], integrals, jnp.zeros_like(integrals))
    fitted = jnp.einsum("jpc,pq->jqc", masked, metric_factor, preferred_element_type=jnp.float32)
    return fitted.astype(jnp.bfloat16)


def body(integrals, metric_factor, coefficients, owners, row_block, column_block, screen_counts):
    n_aux = lax.axis_size("aux")
    here = lax.axis_index("aux")
    slots = integrals.shape[0]
    aux_local = integrals.shape[1]
    all_owners = owners[:, 0].reshape(n_aux, slots)
    all_rows = row_block.reshape(n_aux, slots)
    all_cols = column_block.reshape(n_aux, slots)
    earlier = (
        jnp.arange(slots, dtype=jnp.int32)[:, None] > jnp.arange(slots, dtype=jnp.int32)[None, :]
    )
    slot_rank = jnp.sum(
        ((all_owners[:, :, None] == all_owners[:, None, :]) & earlier[None]).astype(jnp.int32),
        axis=2,
    )
    mine_owners = lax.dynamic_index_in_dim(all_owners, here, 0, keepdims=False)
    mine_rank = lax.dynamic_index_in_dim(slot_rank, here, 0, keepdims=False)
    local_counts = lax.dynamic_slice_in_dim(screen_counts, here * slots, slots)
    fitted = fit_slab(integrals, metric_factor, local_counts)
    gathered = lax.all_gather(coefficients, "occ", axis=1, tiled=True)
    occ_all = gathered.shape[1]
    scale = 1.0 / (occ_all * aux_local)
    target = mine_owners * CAP + mine_rank
    placing = (jnp.arange(n_aux * CAP, dtype=jnp.int32)[:, None] == target[None, :]).astype(
        jnp.bfloat16
    )
    outgoing = jnp.dot(placing, fitted.reshape(slots, -1), preferred_element_type=jnp.float32)
    outgoing = outgoing.astype(jnp.bfloat16).reshape(n_aux, CAP, aux_local, BF * BF)
    received = lax.all_to_all(outgoing, "aux", split_axis=0, concat_axis=0, tiled=True)
    matching = (all_owners == here)[:, None, :] & (
        slot_rank[:, None, :] == jnp.arange(CAP, dtype=jnp.int32)[None, :, None]
    )
    source_cols = jnp.sum(jnp.where(matching, all_cols[:, None, :], 0), axis=2)
    source_rows = jnp.sum(jnp.where(matching, all_rows[:, None, :], 0), axis=2)
    present = jnp.any(matching, axis=2)
    weights = (
        (source_rows[:, None, :] == jnp.arange(NBLK_DEV, dtype=jnp.int32)[None, :, None])
        & present[:, None, :]
    ).astype(jnp.bfloat16)

    def per_source(total, inputs):
        pieces, columns, weight_rows = inputs
        halves = []
        for turn in range(CAP):
            rows_here = lax.dynamic_slice_in_dim(gathered, columns[turn] * BF, BF, 0)
            product = jnp.dot(
                pieces[turn].reshape(aux_local * BF, BF),
                rows_here,
                preferred_element_type=jnp.float32,
            )
            halves.append(product.astype(jnp.bfloat16).reshape(-1))
        stacked = jnp.stack(halves)
        grouped = jnp.dot(weight_rows, stacked, preferred_element_type=jnp.float32).astype(
            jnp.bfloat16
        )
        grouped = grouped.reshape(NBLK_DEV, aux_local, BF, occ_all)
        return (
            total
            + jnp.einsum("xqmi,xqni->xmn", grouped, grouped, preferred_element_type=jnp.float32),
            None,
        )

    start = jnp.zeros((NBLK_DEV, BF, BF), jnp.float32)
    total, _ = lax.scan(per_source, start, (received, source_cols, weights))
    summed = lax.psum(total, "occ")
    return summed.reshape(NBLK_DEV, BF * BF) * scale


def solution(mesh):
    return jax.shard_map(
        body,
        mesh=mesh,
        in_specs=(
            P("aux", "occ", None),
            P(("aux", "occ"), None),
            P(None, "occ"),
            P(),
            P(),
            P(),
            P(),
        ),
        out_specs=P("aux", None),
        check_vma=False,
    )
```

profile of v0, /device:TPU:0, one launch (start us, length us, event | category | flops | bytes accessed | tf_op | source)
XLA Modules:
  0.0 214.6 jit_solution(16433242171921053069)
XLA Ops:
  7.4 3.6 %convolution_convert_fusion.4 = bf16[16,16384,8]{1,2,0:T(8,128)(2,1)S(1)} fusion(bf16[16,8,16384]{2,1,0:T(8,128)(2,1)} %param.9, pred[16,8]{1,0:T(8,128)(4,1)S(1)} %iota_compare_fusion, bf16[8,8]{1,0:T(8,128)(2,1)S(1)} %copy-done), kind=kOutput, calls=%fused_computation.23 | convolution fusion | flops 37748736 | bytes 8388864 | tf_op jit(solution)/shard_map/jpc,pq->jqc/dot_general | solution.py:15
  10.9 4.2 %copy.22 = bf16[2,8,8,16384]{3,1,2,0:T(8,128)(2,1)} copy(bf16[2,8,8,16384]{3,2,1,0:T(8,128)(2,1)S(1)} %bitcast.80) | data formatting | bytes 8388608
  16.7 3.4 %convolution_convert_fusion.3 = bf16[16,131072]{1,0:T(8,128)(2,1)S(1)} fusion(bf16[16,131072]{1,0:T(8,128)(2,1)} %bitcast.77, s32[16]{0:T(128)S(1)} %add_bitcast_fusion), kind=kOutput, calls=%fused_computation.22 | convolution fusion | flops 69206272 | bytes 8388672 | tf_op jit(solution)/shard_map/dot_general | solution.py:45
  20.2 4.3 %copy.23 = bf16[2,8,8,16384]{3,2,1,0:T(8,128)(2,1)} copy(bf16[2,8,8,16384]{3,1,2,0:T(8,128)(2,1)S(1)} %bitcast.78) | data formatting | bytes 8388608
  24.4 7.4 %all-to-all-start = ((bf16[8,2,8,16384]{3,2,1,0:T(8,128)(2,1)}), bf16[8,2,8,16384]{3,2,1,0:T(8,128)(2,1)}, u32[]{:S(2)}, u32[]{:S(2)}) async-start(bf16[8,2,8,16384]{3,2,1,0:T(8,128)(2,1)} %bitcast.79), calls=%async_computation | async-start | bytes 8388608 | tf_op jit(solution)/shard_map/all_to_all | solution.py:47
  32.6 7.3 %all_gather.3 = bf16[2048,128]{0,1:T(8,128)(2,1)S(1)} all-gather(bf16[2048,32]{0,1:T(8,128)(2,1)S(1)} %copy-done.2), channel_id=1, replica_groups=mesh['aux'=8,'occ'=4] {'occ'}, dimensions={1}, use_global_device_ids=true | all-gather | bytes 655360 | tf_op jit(solution)/shard_map/all_gather | solution.py:38
  40.2 84.9 %all-to-all-done = bf16[8,2,8,16384]{3,2,1,0:T(8,128)(2,1)} async-done(((bf16[8,2,8,16384]{3,2,1,0:T(8,128)(2,1)}), bf16[8,2,8,16384]{3,2,1,0:T(8,128)(2,1)}, u32[]{:S(2)}, u32[]{:S(2)}) %all-to-all-start) | async-done | bytes 4194336 | tf_op jit(solution)/shard_map/all_to_all | solution.py:47
  125.1 49.7 %while.11 = (s32[]{:T(128)}, f32[2,128,128]{2,1,0:T(8,128)S(1)}, bf16[8,2,2]{2,1,0:T(2,128)(2,1)S(1)}, bf16[8,2,8,16384]{3,2,1,0:T(8,128)(2,1)}, s32[8,2]{0,1:T(...) while((s32[]{:T(128)}, f32[2,128,128]{2,1,0:T(8,128)S(1)}, ...), condition=%wide.region_5.6_spmd.clone, body=%wide.region_4.5_spmd.clone.sunk | while | flops 136904704 | bytes 7668503 | solution.py:82
  126.4 1.1 constant_dynamic-slice_fusion.6
  129.6 1.3 fusion.48
  132.6 1.1 constant_dynamic-slice_fusion.6
  135.8 1.3 fusion.48
  138.7 1.1 constant_dynamic-slice_fusion.6
  142.0 1.3 fusion.48
  145.0 1.1 constant_dynamic-slice_fusion.6
  148.2 1.3 fusion.48
  151.2 1.1 constant_dynamic-slice_fusion.6
  154.4 1.3 fusion.48
  157.4 1.1 constant_dynamic-slice_fusion.6
  160.6 1.3 fusion.48
  163.6 1.1 constant_dynamic-slice_fusion.6
  166.8 1.3 fusion.48
  173.1 1.3 fusion.48
  175.5 30.6 %all-reduce.2.cloned.1.call-done = f32[2,128,128]{2,1,0:T(8,128)} async-done(((f32[2,128,128]{2,1,0:T(8,128)}), f32[2,128,128]{2,1,0:T(8,128)}) %all-reduce.2.cloned.1.call-update) | async-done | bytes 131088 | tf_op jit(solution)/shard_map/psum | solution.py:83
  (107 shorter events, 26.7 us)
Async XLA Ops:
  6.5 0.8 copy-start
  10.9 4.7 %copy-start.5 = (s32[128,1]{0,1:T(1,128)S(1)}, s32[128,1]{0,1:T(1,128)}, u32[]{:S(2)}) copy-start(s32[128,1]{0,1:T(1,128)} %param.12) | copy-start | bytes 1540
  24.4 7.5 %copy-start.3 = (s32[128]{0:T(128)S(1)}, s32[128]{0:T(128)}, u32[]{:S(2)}) copy-start(s32[128]{0:T(128)} %param.13) | copy-start | bytes 1540
  24.4 7.6 %copy-start.4 = (s32[128]{0:T(128)S(1)}, s32[128]{0:T(128)}, u32[]{:S(2)}) copy-start(s32[128]{0:T(128)} %param.14) | copy-start | bytes 1540
  24.4 8.1 %copy-start.2 = (bf16[2048,32]{0,1:T(8,128)(2,1)S(1)}, bf16[2048,32]{0,1:T(8,128)(2,1)}, u32[]{:S(2)}) copy-start(bf16[2048,32]{0,1:T(8,128)(2,1)} %param.11) | copy-start | bytes 393220
  24.4 100.7 %all-to-all-start = ((bf16[8,2,8,16384]{3,2,1,0:T(8,128)(2,1)}), bf16[8,2,8,16384]{3,2,1,0:T(8,128)(2,1)}, u32[]{:S(2)}, u32[]{:S(2)}) async-start(bf16[8,2,8,16384]{3,2,1,0:T(8,128)(2,1)} %bitcast.79), calls=%async_computation | async-start | bytes 8388608 | tf_op jit(solution)/shard_map/all_to_all | solution.py:47
  31.8 174.2 %all-reduce.2.cloned.1.call-start = ((), (), s32[]{:S(2)}) async-start(), calls=%async_computation.1 | async-start | bytes 262144 | tf_op jit(solution)/shard_map/psum | solution.py:83
  174.8 0.7 copy-start.1
Sparse Core Ops, SparseCore 0:
  175.6 30.4 all-reduce.1
where the time goes:
time: 215 us
  waiting for transfers between devices  116 us (54%)
  local copies, waits for them, and re-layouts  34.4 us (16%)
  matrix products  23.5 us (11%)
  between operations  13.5 us (6%)
  loops' own time  10.6 us (5%)
  starting transfers between devices  7.45 us (3%)
  blocking collectives  7.35 us (3%)
  other arithmetic  2.29 us (1%)
    all_to_all x1, waiting for transfers between devices, body(): lax.all_to_all(outgoing, 'aux', split_axis=0, concat_axis=0, tiled=True)  84.9 us
    psum x1, waiting for transfers between devices, body(): summed = lax.psum(total, 'occ')  30.6 us
    unnamed x17, local copies, waits for them, and re-layouts  10.7 us
    another operation x1, loops' own time, body(): total, _ = lax.scan(per_source, start, (received, source_cols, weights))  10.6 us
    dot_general x8, matrix products, per_source(): jnp.dot(weight_rows, stacked, preferred_element_type=jnp.float32)  10.5 us
    slice x8, local copies, waits for them, and re-layouts, per_source(): pieces[turn].reshape(aux_local * BF, BF)  8.57 us
    all_to_all x1, starting transfers between devices, body(): lax.all_to_all(outgoing, 'aux', split_axis=0, concat_axis=0, tiled=True)  7.41 us
    all_gather x1, blocking collectives, body(): gathered = lax.all_gather(coefficients, 'occ', axis=1, tiled=True)  7.35 us
  transfers between devices with their start and end apart: 2, of which 2 were waited for; matrix products, arithmetic and copies ran while one was open for 0% of the time, Pallas kernels for 0%

commit v1 on v0

v1 whole, which is shorter than its diff:
```python
import functools

import jax
import jax.numpy as jnp
from jax import lax
from jax.experimental import pallas as pl
from jax.experimental.pallas import tpu as pltpu
from jax.sharding import PartitionSpec as P

BF = 128
NBLK_DEV = 2
CORES = 2
EXTRA = 8
LAG1 = 3
LAG2 = 6
MESH = pl.DeviceIdType.MESH
NT = (((1,), (1,)), ((), ()))


def kernel(
    n_aux, n_occ, owners, rows_in, cols_in, counts,
    x_hbm, factor, coef_hbm, out,
    x, fit, coef, mix, part, r1, held, r2, mine, r3, fin,
    x_sem, c_local, c_send, c_recv, s1, v1, s2, v2, s3, v3, s4, v4,
):
    slots, stacked, _ = x.shape
    aux_local = factor.shape[0]
    occ_local = coef_hbm.shape[0]
    occ_all = n_occ * occ_local
    n_x = n_occ // CORES
    chunk = BF // n_occ
    group = 256 // aux_local
    scale = 1.0 / (occ_all * aux_local)
    me, oc = lax.axis_index("aux"), lax.axis_index("occ")
    mx, mc = lax.div(oc, CORES), lax.rem(oc, CORES)
    spot = mc * n_x + mx

    def x_copy(j):
        return pltpu.make_async_copy(x_hbm.at[j], x.at[j], x_sem.at[j])

    def own_coef(b):
        return pltpu.make_async_copy(
            coef_hbm.at[:, b * BF:(b + 1) * BF], coef.at[oc, b], c_local.at[b])

    for b in range(coef.shape[1]):
        own_coef(b).start()
    for j in range(slots):
        x_copy(j).start()

    barrier = pltpu.get_barrier_semaphore()
    for e in range(1, n_occ):
        pl.semaphore_signal(barrier, inc=1, device_id=(me, lax.rem(oc + e, n_occ)), device_id_type=MESH)
    for k in range(n_aux - 1):
        pl.semaphore_signal(barrier, inc=1, device_id=(lax.rem(me + 1 + k, n_aux), oc), device_id_type=MESH)
    pl.semaphore_wait(barrier, n_occ - 1 + n_aux - 1)

    def c_copy(e):
        return pltpu.make_async_remote_copy(
            src_ref=coef.at[oc], dst_ref=coef.at[oc],
            send_sem=c_send.at[e - 1], recv_sem=c_recv.at[e - 1],
            device_id=(me, lax.rem(oc + e, n_occ)), device_id_type=MESH)

    for b in range(coef.shape[1]):
        own_coef(b).wait()
    for e in range(1, n_occ):
        c_copy(e).start()

    side = group * aux_local
    r = lax.broadcasted_iota(jnp.int32, (side, aux_local), 0)
    q = lax.broadcasted_iota(jnp.int32, (side, aux_local), 1)
    spread = jnp.where(r // group == q, 1.0, 0.0).astype(jnp.bfloat16)
    left = lax.dot_general(spread, factor[...], NT, preferred_element_type=jnp.float32).astype(jnp.bfloat16)
    spread = jnp.where(r % aux_local == q, 1.0, 0.0).astype(jnp.bfloat16)
    both = lax.dot_general(left, spread, NT, preferred_element_type=jnp.float32)
    r = lax.broadcasted_iota(jnp.int32, (side, side), 0)
    q = lax.broadcasted_iota(jnp.int32, (side, side), 1)
    mix[...] = jnp.where(r % group == q // aux_local, both, 0.0).astype(jnp.bfloat16)
    aux_of = lax.broadcasted_iota(jnp.int32, (1, side), 1) % aux_local

    def fit_one(j, _):
        x_copy(j).wait()
        live = jnp.where(aux_of < counts[me * slots + j], 1.0, 0.0).astype(jnp.bfloat16)
        factors = mix[...] * live
        for g in range(stacked // side):
            f = jnp.dot(factors, x[j, g * side:(g + 1) * side, :], preferred_element_type=jnp.float32)
            fit[j, :, g * group:(g + 1) * group, :] = f.astype(jnp.bfloat16).reshape(aux_local, group, BF)
        return 0

    lax.fori_loop(0, slots, fit_one, 0)

    for e in range(1, n_occ):
        c_copy(e).wait_recv()

    rr = lax.broadcasted_iota(jnp.int32, (BF, BF), 0)
    cc = lax.broadcasted_iota(jnp.int32, (BF, BF), 1)

    def compute(k):
        w = lax.rem(me + 1 + k, n_aux)
        j1, j2 = jnp.int32(slots), jnp.int32(-1)
        for j in range(slots):
            hit = owners[me * slots + j] == w
            j1 = jnp.where(hit, jnp.minimum(j1, j), j1)
            j2 = jnp.where(hit, j, j2)
        p1 = j2 >= 0
        p2 = jnp.logical_and(p1, j1 != j2)
        j1, j2 = jnp.where(p1, j1, 0), jnp.where(p1, j2, 0)
        row1, row2 = rows_in[me * slots + j1], rows_in[me * slots + j2]
        b1, b2 = cols_in[me * slots + j1], cols_in[me * slots + j2]
        f = jnp.concatenate([fit[j1].reshape(aux_local * BF, BF), fit[j2].reshape(aux_local * BF, BF)], axis=1)
        c1 = jnp.concatenate([coef[o, b1] for o in range(n_occ)], axis=0)
        c2 = jnp.concatenate([coef[o, b2] for o in range(n_occ)], axis=0)

        def weigh(c, present, row, which):
            on = jnp.where(jnp.logical_and(present, row == which), 1.0, 0.0)
            return c * on.astype(jnp.bfloat16)

        weights = jnp.concatenate([
            jnp.concatenate([weigh(c1, p1, row1, which), weigh(c2, p2, row2, which)], axis=1)
            for which in range(NBLK_DEV)], axis=0)
        grouped = lax.dot_general(f, weights, NT, preferred_element_type=jnp.float32).astype(jnp.bfloat16)
        squares = []
        for which in range(NBLK_DEV):
            g = jnp.concatenate([
                grouped[a * BF:(a + 1) * BF, which * occ_all:(which + 1) * occ_all]
                for a in range(aux_local)], axis=1)
            squares.append(lax.dot_general(g, g, NT, preferred_element_type=jnp.float32) * scale)
        packed = jnp.where(rr >= cc, squares[0], squares[1])
        diag = jnp.sum(jnp.where(rr == cc, squares[1], 0.0), axis=0, keepdims=True)
        tail = jnp.broadcast_to(diag, (EXTRA, BF))
        for c in range(CORES):
            for i in range(n_x):
                at = (c * n_x + i) * chunk
                part[k, c, i, 0:chunk, :] = packed[at:at + chunk]
                part[k, c, i, chunk:chunk + EXTRA, :] = tail

    def copy1(k):
        return pltpu.make_async_remote_copy(
            src_ref=part.at[k, 1 - mc], dst_ref=r1.at[k],
            send_sem=s1.at[k], recv_sem=v1.at[k],
            device_id=(me, mx * CORES + 1 - mc), device_id_type=MESH)

    def copy2(k, d):
        to = lax.rem(mx + d, n_x)
        return pltpu.make_async_remote_copy(
            src_ref=held.at[k, to], dst_ref=r2.at[k, d - 1],
            send_sem=s2.at[k, d - 1], recv_sem=v2.at[k, d - 1],
            device_id=(me, to * CORES + mc), device_id_type=MESH)

    def copy3(k):
        return pltpu.make_async_remote_copy(
            src_ref=mine.at[k], dst_ref=r3.at[k],
            send_sem=s3.at[k], recv_sem=v3.at[k],
            device_id=(lax.rem(me + 1 + k, n_aux), oc), device_id_type=MESH)

    def copy4(e):
        return pltpu.make_async_remote_copy(
            src_ref=fin.at[spot], dst_ref=fin.at[spot],
            send_sem=s4.at[e - 1], recv_sem=v4.at[e - 1],
            device_id=(me, lax.rem(oc + e, n_occ)), device_id_type=MESH)

    def step(t, _):
        @pl.when(t < n_aux)
        def _():
            compute(t)
            copy1(t).start()

        @pl.when(jnp.logical_and(t >= LAG1, t < n_aux + LAG1))
        def _():
            k = t - LAG1
            copy1(k).wait_recv()
            held[k] = part[k, mc] + r1[k]
            for d in range(1, n_x):
                copy2(k, d).start()

        @pl.when(t >= LAG2)
        def _():
            k = t - LAG2
            total = held[k, mx]
            for d in range(1, n_x):
                copy2(k, d).wait_recv()
                total = total + r2[k, d - 1]
            mine[k] = total

            @pl.when(k < n_aux - 1)
            def _():
                copy3(k).start()
        return 0

    lax.fori_loop(0, n_aux + LAG2, step, 0)

    def gather3(k, total):
        copy3(k).wait_recv()
        return total + r3[k]

    fin[spot] = lax.fori_loop(0, n_aux - 1, gather3, mine[n_aux - 1])
    for e in range(1, n_occ):
        copy4(e).start()

    def drain(k, _):
        copy1(k).wait_send()
        for d in range(1, n_x):
            copy2(k, d).wait_send()

        @pl.when(k < n_aux - 1)
        def _():
            copy3(k).wait_send()
        return 0

    lax.fori_loop(0, n_aux, drain, 0)
    for e in range(1, n_occ):
        c_copy(e).wait_send()
    for e in range(1, n_occ):
        copy4(e).wait_recv()
    whole = jnp.concatenate([fin[i, 0:chunk, :] for i in range(n_occ)], axis=0)
    turned = whole.T
    out[0] = jnp.where(rr >= cc, whole, turned)
    out[1] = jnp.where(rr == cc, fin[0, chunk:chunk + 1, :], jnp.where(rr < cc, whole, turned))
    for e in range(1, n_occ):
        copy4(e).wait_send()


def body(integrals, metric_factor, coefficients, owners, row_block, column_block, screen_counts):
    n_aux, n_occ = lax.axis_size("aux"), lax.axis_size("occ")
    slots, aux_local, flat = integrals.shape
    nbasis, occ_local = coefficients.shape
    stacked = integrals.reshape(slots, aux_local, BF, BF).transpose(0, 2, 1, 3).reshape(slots, aux_local * BF, BF)
    n_x = n_occ // CORES
    rows = BF // n_occ + EXTRA
    occ_all = n_occ * occ_local
    dma = pltpu.SemaphoreType.DMA
    f32, bf16 = jnp.float32, jnp.bfloat16
    smem = pl.BlockSpec(memory_space=pltpu.SMEM)
    vmem = pl.BlockSpec(memory_space=pltpu.VMEM)
    hbm = pl.BlockSpec(memory_space=pl.ANY)
    flops = 2 * slots * aux_local * BF * (256 * BF + 2 * BF * occ_all)
    out = pl.pallas_call(
        functools.partial(kernel, n_aux, n_occ),
        out_shape=jax.ShapeDtypeStruct((NBLK_DEV, BF, BF), f32),
        in_specs=[smem] * 4 + [hbm, vmem, hbm],
        out_specs=vmem,
        scratch_shapes=[
            pltpu.VMEM((slots, aux_local * BF, BF), bf16),
            pltpu.VMEM((slots, aux_local, BF, BF), bf16),
            pltpu.VMEM((n_occ, nbasis // BF, occ_local, BF), bf16),
            pltpu.VMEM((256, 256), bf16),
            pltpu.VMEM((n_aux, CORES, n_x, rows, BF), f32),
            pltpu.VMEM((n_aux, n_x, rows, BF), f32),
            pltpu.VMEM((n_aux, n_x, rows, BF), f32),
            pltpu.VMEM((n_aux, n_x - 1, rows, BF), f32),
            pltpu.VMEM((n_aux, rows, BF), f32),
            pltpu.VMEM((n_aux - 1, rows, BF), f32),
            pltpu.VMEM((n_occ, rows, BF), f32),
            dma((slots,)), dma((nbasis // BF,)),
            dma((n_occ - 1,)), dma((n_occ - 1,)),
            dma((n_aux,)), dma((n_aux,)),
            dma((n_aux, n_x - 1)), dma((n_aux, n_x - 1)),
            dma((n_aux - 1,)), dma((n_aux - 1,)),
            dma((n_occ - 1,)), dma((n_occ - 1,)),
        ],
        compiler_params=pltpu.CompilerParams(
            collective_id=0, has_side_effects=True, vmem_limit_bytes=61 * 1024 * 1024),
        cost_estimate=pl.CostEstimate(
            flops=flops, bytes_accessed=integrals.size * 2, transcendentals=0),
    )(owners.reshape(-1), row_block, column_block, screen_counts, stacked, metric_factor, coefficients.T)
    return out.reshape(NBLK_DEV, BF * BF)


def solution(mesh):
    return jax.shard_map(
        body,
        mesh=mesh,
        in_specs=(
            P("aux", "occ", None),
            P(("aux", "occ"), None),
            P(None, "occ"),
            P(),
            P(),
            P(),
            P(),
        ),
        out_specs=P("aux", None),
        check_vma=False,
    )
```

time: 215 us -> 32 us (0.15)
  waiting for transfers between devices: 116 us -> 0 us
  local copies, waits for them, and re-layouts: 34.4 us -> 1.66 us
  Pallas kernels: 0 us -> 30.1 us
  matrix products: 23.5 us -> 0 us
  between operations: 13.5 us -> 0.01 us
  loops' own time: 10.6 us -> 0 us
  starting transfers between devices: 7.45 us -> 0 us
  blocking collectives: 7.35 us -> 0 us
  other arithmetic: 2.29 us -> 0 us
    all_to_all x1 -> x0, waiting for transfers between devices: 84.9 us -> none  [body(): lax.all_to_all(outgoing, 'aux', split_axis=0, concat_axis=0, tiled=True)]
    psum x1 -> x0, waiting for transfers between devices: 30.6 us -> none  [body(): summed = lax.psum(total, 'occ')]
    pallas_call x0 -> x1, Pallas kernels: none -> 30.1 us  [body(): pl.pallas_call(functools.partial(kernel, n_aux, n_occ), out_shape=jax.Sha...]
    dot_general x34 -> x0, matrix products: 23.5 us -> none  [the longest x8 10.5 us: per_source(): jnp.dot(weight_rows, stacked, preferred_element_type=jnp.float32)]
    slice x16 -> x0, local copies, waits for them, and re-layouts: 13 us -> none  [the longest x8 8.57 us: per_source(): pieces[turn].reshape(aux_local * BF, BF)]
    another operation x1 -> x0, loops' own time: 10.6 us -> none  [body(): total, _ = lax.scan(per_source, start, (received, source_cols, weights))]
    unnamed x17 -> x1, local copies, waits for them, and re-layouts: 10.7 us -> 1.66 us
    all_to_all x1 -> x0, starting transfers between devices: 7.41 us -> none  [body(): lax.all_to_all(outgoing, 'aux', split_axis=0, concat_axis=0, tiled=True)]
  transfers between devices with their start and end apart: 2 -> 0, of which waited for: 2 -> 0; matrix products, arithmetic and copies ran while one was open for 0% -> 0% of each run, Pallas kernels for 0% -> 0%
where the time goes in v1:
time: 32 us; the launch traced here: 31.8 us
  Pallas kernels  30.1 us (94%)
  local copies, waits for them, and re-layouts  1.66 us (5%)
    pallas_call x1, Pallas kernels, body(): pl.pallas_call(functools.partial(kernel, n_aux, n_occ), out_shape=jax.Sha...  30.1 us
    unnamed x1, local copies, waits for them, and re-layouts  1.66 us

profile of v1, /device:TPU:0, one launch (start us, length us, event | category | flops | bytes accessed | tf_op | source)
XLA Modules:
  0.0 31.8 jit_solution(15582816566290720783)
XLA Ops:
  0.0 30.1 %shard_map.73 = f32[2,128,128]{2,1,0:T(8,128)} custom-call(s32[128]{0:T(128)} %bitcast.14, s32[128]{0:T(128)} %rows_in.1, s32[128]{0:T(128)} %cols_in.1, s32[128]{0:T(128)} %counts.1, bf16[16,1024,128]{2,1,0:T(8,128)(2,1)} %bitcast.12, bf16[8,8]{1,0:T(8,128)(2,1)} %factor.1, bf16[32,2048]{1,0:T(8,128)(2,1)} %bitcast.13), custom_call_target="tpu_custom_call" | custom-call | flops 2147483648 | bytes 4194304 | tf_op jit(solution)/shard_map/pallas_call | solution.py:236
  30.1 1.7 %copy.10 = f32[1,2,128,128]{3,1,2,0:T(2,128)} copy(f32[1,2,128,128]{3,2,1,0:T(8,128)} %bitcast.11) | data formatting | bytes 262144

commit v2 on v1

--- a/solution.py
+++ b/solution.py
@@ -18,8 +18,9 @@
 
 
 def kernel(
-    n_aux, n_occ, owners, rows_in, cols_in, counts,
-    x_hbm, factor, coef_hbm, out,
+    n_aux, n_occ, owners_hbm, rows_hbm, cols_hbm, counts_hbm,
+    x_hbm, factor_hbm, coef_hbm, out,
+    owners, rows_in, cols_in, counts, factor, small_sem,
     x, fit, coef, mix, part, r1, held, r2, mine, r3, fin,
     x_sem, c_local, c_send, c_recv, s1, v1, s2, v2, s3, v3, s4, v4,
 ):
@@ -44,6 +45,13 @@
 
     for b in range(coef.shape[1]):
         own_coef(b).start()
+    small = [
+        pltpu.make_async_copy(a, b, small_sem.at[i])
+        for i, (a, b) in enumerate([
+            (factor_hbm, factor), (counts_hbm, counts), (owners_hbm, owners),
+            (rows_hbm, rows_in), (cols_hbm, cols_in)])]
+    for copy in small:
+        copy.start()
     for j in range(slots):
         x_copy(j).start()
 
@@ -55,15 +63,24 @@
     pl.semaphore_wait(barrier, n_occ - 1 + n_aux - 1)
 
     def c_copy(e):
-        return pltpu.make_async_remote_copy(
-            src_ref=coef.at[oc], dst_ref=coef.at[oc],
-            send_sem=c_send.at[e - 1], recv_sem=c_recv.at[e - 1],
-            device_id=(me, lax.rem(oc + e, n_occ)), device_id_type=MESH)
+        if e == 0:
+            what, to = oc, mx * CORES + 1 - mc
+        elif e < n_x:
+            what, to = oc, lax.rem(mx + e, n_x) * CORES + mc
+        else:
+            what, to = lax.rem(mx + e + 1, n_x) * CORES + mc, mx * CORES + 1 - mc
+        return pltpu.make_async_remote_copy(
+            src_ref=coef.at[what], dst_ref=coef.at[what],
+            send_sem=c_send.at[e], recv_sem=c_recv.at[e],
+            device_id=(me, to), device_id_type=MESH)
 
     for b in range(coef.shape[1]):
         own_coef(b).wait()
-    for e in range(1, n_occ):
+    for e in list(range(1, n_x)) + [0]:
         c_copy(e).start()
+
+    for copy in small:
+        copy.wait()
 
     side = group * aux_local
     r = lax.broadcasted_iota(jnp.int32, (side, aux_local), 0)
@@ -86,9 +103,15 @@
             fit[j, :, g * group:(g + 1) * group, :] = f.astype(jnp.bfloat16).reshape(aux_local, group, BF)
         return 0
 
-    lax.fori_loop(0, slots, fit_one, 0)
-
-    for e in range(1, n_occ):
+    before = slots * 3 // 4
+    lax.fori_loop(0, before, fit_one, 0)
+    for e in range(1, n_x):
+        c_copy(e).wait_recv()
+    for e in range(n_x, n_occ - 1):
+        c_copy(e).start()
+    lax.fori_loop(before, slots, fit_one, 0)
+    c_copy(0).wait_recv()
+    for e in range(n_x, n_occ - 1):
         c_copy(e).wait_recv()
 
     rr = lax.broadcasted_iota(jnp.int32, (BF, BF), 0)
@@ -207,7 +230,7 @@
         return 0
 
     lax.fori_loop(0, n_aux, drain, 0)
-    for e in range(1, n_occ):
+    for e in range(n_occ - 1):
         c_copy(e).wait_send()
     for e in range(1, n_occ):
         copy4(e).wait_recv()
@@ -229,16 +252,21 @@
     occ_all = n_occ * occ_local
     dma = pltpu.SemaphoreType.DMA
     f32, bf16 = jnp.float32, jnp.bfloat16
-    smem = pl.BlockSpec(memory_space=pltpu.SMEM)
     vmem = pl.BlockSpec(memory_space=pltpu.VMEM)
     hbm = pl.BlockSpec(memory_space=pl.ANY)
     flops = 2 * slots * aux_local * BF * (256 * BF + 2 * BF * occ_all)
     out = pl.pallas_call(
         functools.partial(kernel, n_aux, n_occ),
         out_shape=jax.ShapeDtypeStruct((NBLK_DEV, BF, BF), f32),
-        in_specs=[smem] * 4 + [hbm, vmem, hbm],
+        in_specs=[hbm] * 7,
         out_specs=vmem,
         scratch_shapes=[
+            pltpu.SMEM(row_block.shape, jnp.int32),
+            pltpu.SMEM(row_block.shape, jnp.int32),
+            pltpu.SMEM(row_block.shape, jnp.int32),
+            pltpu.SMEM(row_block.shape, jnp.int32),
+            pltpu.VMEM(metric_factor.shape, bf16),
+            dma((5,)),
             pltpu.VMEM((slots, aux_local * BF, BF), bf16),
             pltpu.VMEM((slots, aux_local, BF, BF), bf16),
             pltpu.VMEM((n_occ, nbasis // BF, occ_local, BF), bf16),

time: 32 us -> 30.6 us (0.956)
  Pallas kernels: 30.1 us -> 28.8 us
    pallas_call x1, Pallas kernels: 30.1 us -> 28.8 us  [body(): pl.pallas_call(functools.partial(kernel, n_aux, n_occ), out_shape=jax.Sha...]
where the time goes in v2:
time: 30.6 us; the launch traced here: 30.5 us
  Pallas kernels  28.8 us (94%)
  local copies, waits for them, and re-layouts  1.66 us (5%)
    pallas_call x1, Pallas kernels, body(): pl.pallas_call(functools.partial(kernel, n_aux, n_occ), out_shape=jax.Sha...  28.8 us
    unnamed x1, local copies, waits for them, and re-layouts  1.66 us

profile of v2, /device:TPU:0, one launch (start us, length us, event | category | flops | bytes accessed | tf_op | source)
XLA Modules:
  0.0 30.5 jit_solution(9412205862308612370)
XLA Ops:
  0.0 28.8 %shard_map.73 = f32[2,128,128]{2,1,0:T(8,128)} custom-call(s32[128]{0:T(128)} %bitcast.14, s32[128]{0:T(128)} %rows_hbm.1, s32[128]{0:T(128)} %cols_hbm.1, s32[128]{0:T(128)} %counts_hbm.1, bf16[16,1024,128]{2,1,0:T(8,128)(2,1)} %bitcast.12, bf16[8,8]{1,0:T(8,128)(2,1)} %factor_hbm.1, bf16[32,2048]{1,0:T(8,128)(2,1)} %bitcast.13), custom_call_target="tpu_custom_call" | custom-call | flops 2147483648 | bytes 4194304 | tf_op jit(solution)/shard_map/pallas_call | solution.py:258
  28.8 1.7 %copy.10 = f32[1,2,128,128]{3,1,2,0:T(2,128)} copy(f32[1,2,128,128]{3,2,1,0:T(8,128)} %bitcast.11) | data formatting | bytes 262144

commit v3 on v2

--- a/solution.py
+++ b/solution.py
@@ -11,8 +11,8 @@
 NBLK_DEV = 2
 CORES = 2
 EXTRA = 8
-LAG1 = 3
-LAG2 = 6
+LAG1 = 1
+LAG2 = 3
 MESH = pl.DeviceIdType.MESH
 NT = (((1,), (1,)), ((), ()))
 
@@ -60,7 +60,6 @@
         pl.semaphore_signal(barrier, inc=1, device_id=(me, lax.rem(oc + e, n_occ)), device_id_type=MESH)
     for k in range(n_aux - 1):
         pl.semaphore_signal(barrier, inc=1, device_id=(lax.rem(me + 1 + k, n_aux), oc), device_id_type=MESH)
-    pl.semaphore_wait(barrier, n_occ - 1 + n_aux - 1)
 
     def c_copy(e):
         if e == 0:
@@ -74,10 +73,6 @@
             send_sem=c_send.at[e], recv_sem=c_recv.at[e],
             device_id=(me, to), device_id_type=MESH)
 
-    for b in range(coef.shape[1]):
-        own_coef(b).wait()
-    for e in list(range(1, n_x)) + [0]:
-        c_copy(e).start()
 
     for copy in small:
         copy.wait()
@@ -103,8 +98,15 @@
             fit[j, :, g * group:(g + 1) * group, :] = f.astype(jnp.bfloat16).reshape(aux_local, group, BF)
         return 0
 
-    before = slots * 3 // 4
-    lax.fori_loop(0, before, fit_one, 0)
+    early = slots * 4 // 16
+    lax.fori_loop(0, early, fit_one, 0)
+    pl.semaphore_wait(barrier, n_occ - 1 + n_aux - 1)
+    for b in range(coef.shape[1]):
+        own_coef(b).wait()
+    for e in list(range(1, n_x)) + [0]:
+        c_copy(e).start()
+    before = slots * 12 // 16
+    lax.fori_loop(early, before, fit_one, 0)
     for e in range(1, n_x):
         c_copy(e).wait_recv()
     for e in range(n_x, n_occ - 1):
@@ -181,35 +183,41 @@
             send_sem=s4.at[e - 1], recv_sem=v4.at[e - 1],
             device_id=(me, lax.rem(oc + e, n_occ)), device_id_type=MESH)
 
+    pairs = n_aux // 2
+
     def step(t, _):
-        @pl.when(t < n_aux)
+        @pl.when(t < pairs)
         def _():
-            compute(t)
-            copy1(t).start()
-
-        @pl.when(jnp.logical_and(t >= LAG1, t < n_aux + LAG1))
+            compute(2 * t)
+            compute(2 * t + 1)
+            copy1(2 * t).start()
+            copy1(2 * t + 1).start()
+
+        @pl.when(jnp.logical_and(t >= LAG1, t < pairs + LAG1))
         def _():
-            k = t - LAG1
-            copy1(k).wait_recv()
-            held[k] = part[k, mc] + r1[k]
-            for d in range(1, n_x):
-                copy2(k, d).start()
+            for i in range(2):
+                k = 2 * (t - LAG1) + i
+                copy1(k).wait_recv()
+                held[k] = part[k, mc] + r1[k]
+                for d in range(1, n_x):
+                    copy2(k, d).start()
 
         @pl.when(t >= LAG2)
         def _():
-            k = t - LAG2
-            total = held[k, mx]
-            for d in range(1, n_x):
-                copy2(k, d).wait_recv()
-                total = total + r2[k, d - 1]
-            mine[k] = total
-
-            @pl.when(k < n_aux - 1)
-            def _():
-                copy3(k).start()
+            for i in range(2):
+                k = 2 * (t - LAG2) + i
+                total = held[k, mx]
+                for d in range(1, n_x):
+                    copy2(k, d).wait_recv()
+                    total = total + r2[k, d - 1]
+                mine[k] = total
+
+                @pl.when(k < n_aux - 1)
+                def _():
+                    copy3(k).start()
         return 0
 
-    lax.fori_loop(0, n_aux + LAG2, step, 0)
+    lax.fori_loop(0, pairs + LAG2, step, 0)
 
     def gather3(k, total):
         copy3(k).wait_recv()

time: 30.6 us -> 29.1 us (0.951)
  Pallas kernels: 28.8 us -> 27.3 us
    pallas_call x1, Pallas kernels: 28.8 us -> 27.3 us  [body(): pl.pallas_call(functools.partial(kernel, n_aux, n_occ), out_shape=jax.Sha...]
where the time goes in v3:
time: 29.1 us; the launch traced here: 28.9 us
  Pallas kernels  27.3 us (94%)
  local copies, waits for them, and re-layouts  1.66 us (6%)
    pallas_call x1, Pallas kernels, body(): pl.pallas_call(functools.partial(kernel, n_aux, n_occ), out_shape=jax.Sha...  27.3 us
    unnamed x1, local copies, waits for them, and re-layouts  1.66 us

profile of v3, /device:TPU:0, one launch (start us, length us, event | category | flops | bytes accessed | tf_op | source)
XLA Modules:
  0.0 28.9 jit_solution(8099216495645965353)
XLA Ops:
  0.0 27.3 %shard_map.73 = f32[2,128,128]{2,1,0:T(8,128)} custom-call(s32[128]{0:T(128)} %bitcast.14, s32[128]{0:T(128)} %rows_hbm.1, s32[128]{0:T(128)} %cols_hbm.1, s32[128]{0:T(128)} %counts_hbm.1, bf16[16,1024,128]{2,1,0:T(8,128)(2,1)} %bitcast.12, bf16[8,8]{1,0:T(8,128)(2,1)} %factor_hbm.1, bf16[32,2048]{1,0:T(8,128)(2,1)} %bitcast.13), custom_call_target="tpu_custom_call" | custom-call | flops 2147483648 | bytes 4194304 | tf_op jit(solution)/shard_map/pallas_call | solution.py:266
  27.3 1.7 %copy.10 = f32[1,2,128,128]{3,1,2,0:T(2,128)} copy(f32[1,2,128,128]{3,2,1,0:T(8,128)} %bitcast.11) | data formatting | bytes 262144

commit v4 on v3

--- a/solution.py
+++ b/solution.py
@@ -98,7 +98,7 @@
             fit[j, :, g * group:(g + 1) * group, :] = f.astype(jnp.bfloat16).reshape(aux_local, group, BF)
         return 0
 
-    early = slots * 4 // 16
+    early = slots * 2 // 16
     lax.fori_loop(0, early, fit_one, 0)
     pl.semaphore_wait(barrier, n_occ - 1 + n_aux - 1)
     for b in range(coef.shape[1]):
@@ -244,8 +244,8 @@
         copy4(e).wait_recv()
     whole = jnp.concatenate([fin[i, 0:chunk, :] for i in range(n_occ)], axis=0)
     turned = whole.T
-    out[0] = jnp.where(rr >= cc, whole, turned)
-    out[1] = jnp.where(rr == cc, fin[0, chunk:chunk + 1, :], jnp.where(rr < cc, whole, turned))
+    out[:, 0, :] = jnp.where(rr >= cc, whole, turned)
+    out[:, 1, :] = jnp.where(rr == cc, fin[0, chunk:chunk + 1, :], jnp.where(rr < cc, whole, turned))
     for e in range(1, n_occ):
         copy4(e).wait_send()
 
@@ -265,7 +265,7 @@
     flops = 2 * slots * aux_local * BF * (256 * BF + 2 * BF * occ_all)
     out = pl.pallas_call(
         functools.partial(kernel, n_aux, n_occ),
-        out_shape=jax.ShapeDtypeStruct((NBLK_DEV, BF, BF), f32),
+        out_shape=jax.ShapeDtypeStruct((BF, NBLK_DEV, BF), f32),
         in_specs=[hbm] * 7,
         out_specs=vmem,
         scratch_shapes=[
@@ -298,7 +298,7 @@
         cost_estimate=pl.CostEstimate(
             flops=flops, bytes_accessed=integrals.size * 2, transcendentals=0),
     )(owners.reshape(-1), row_block, column_block, screen_counts, stacked, metric_factor, coefficients.T)
-    return out.reshape(NBLK_DEV, BF * BF)
+    return out.transpose(1, 0, 2).reshape(NBLK_DEV, BF * BF)
 
 
 def solution(mesh):

time: 29.1 us -> 28.6 us (0.983)
  Pallas kernels: 27.3 us -> 26.9 us
    pallas_call x1, Pallas kernels: 27.3 us -> 26.9 us  [body(): pl.pallas_call(functools.partial(kernel, n_aux, n_occ), out_shape=jax.Sha...]
where the time goes in v4:
time: 28.6 us; the launch traced here: 28.5 us
  Pallas kernels  26.9 us (94%)
  local copies, waits for them, and re-layouts  1.57 us (5%)
    pallas_call x1, Pallas kernels, body(): pl.pallas_call(functools.partial(kernel, n_aux, n_occ), out_shape=jax.Sha...  26.9 us
    unnamed x1, local copies, waits for them, and re-layouts  1.57 us

profile of v4, /device:TPU:0, one launch (start us, length us, event | category | flops | bytes accessed | tf_op | source)
XLA Modules:
  0.0 28.5 jit_solution(4756169873997448873)
XLA Ops:
  0.0 26.9 %shard_map.73 = f32[128,2,128]{2,1,0:T(2,128)} custom-call(s32[128]{0:T(128)} %bitcast.13, s32[128]{0:T(128)} %rows_hbm.1, s32[128]{0:T(128)} %cols_hbm.1, s32[128]{0:T(128)} %counts_hbm.1, bf16[16,1024,128]{2,1,0:T(8,128)(2,1)} %bitcast.11, bf16[8,8]{1,0:T(8,128)(2,1)} %factor_hbm.1, bf16[32,2048]{1,0:T(8,128)(2,1)} %bitcast.12), custom_call_target="tpu_custom_call" | custom-call | flops 2147483648 | bytes 4194304 | tf_op jit(solution)/shard_map/pallas_call | solution.py:266
  26.9 1.6 %copy.9 = f32[2,16384]{1,0:T(2,128)} copy(f32[2,16384]{1,0:T(2,128)} %bitcast.10) | data formatting | bytes 262144
